TPU v7x, 32 devices: a whole 2x2x4 slice. The times are simulated.
32 devices in a mesh: term: 2 (over y), blk: 16 (over z, x, core).
Axes of the slice: x: 2, y: 2, z: 4, core: 2. Of those that a mesh axis runs over, the one named last changes fastest.
Arguments:
- start_vec: float32 [4, 32, 128, 128], P(None, 'blk', 'term'), may hold values from -6 to 6
- left_env: float32 [8, 32, 128, 128], P('term', 'blk'), may hold values from -0.5 to 0.5
- right_env: float32 [8, 32, 128, 128], P('term', 'blk'), may hold values from -0.5 to 0.5
- local_mpo: float32 [8, 4, 4], P('term'), may hold values from -1 to 1
- term_charge: int32 [8], P('term'), may hold values from -1 to 1, as said below
- sector_sizes: int32 [32], P('blk'), may hold values from 64 to 128, as said below
- sector_ranks: int32 [32], P('blk'), may hold values from 32 to 128, as said below
Outputs:
- coeffs: float32 [2, 8], replicated
- krylov: float32 [4, 32, 128, 128], P(None, 'blk', 'term')
- density: float32 [32, 128, 128], P('blk', 'term')
Inputs may be any that keep to these rules, and one draw needn't show every extreme that they name: `term_charge`: each term moves charge by -1, 0 or +1; some term moves +1 and some -1 in every draw, and some moves 0 when 8 is 3 or more. `sector_sizes`: some sector is full in every draw. `sector_ranks`: no sector keeps more states than it has live, and some sector keeps all 128.
All inputs are finite; a program needn't handle non-finite values.
Results may differ from a plain program's by a relative error of at most 0.0003.
Values sent between devices are 32-bit elements; how exact they have to be, the bound alone decides.
A program may use at most 64 MiB of HBM per device.

v0:
```python
import jax
import jax.numpy as jnp
from jax import lax
from jax.sharding import PartitionSpec as P

KRY = 8


HI = lax.Precision.HIGHEST


def from_behind(value, axis, by):
    devices = lax.axis_size(axis)
    pairs = [(i, i + by) for i in range(devices) if 0 <= i + by < devices]
    return lax.ppermute(value, axis, pairs)


def live_mask(counts, width):
    return (jnp.arange(width, dtype=jnp.int32)[None, :] < counts[:, None]).astype(jnp.float32)


def apply_operator(rows_vec, left_env, right_env, local_mpo, term_charge, row_mask):
    whole = lax.all_gather(rows_vec, "term", axis=2, tiled=True)
    lower_edge = from_behind(whole[:, -1:], "blk", 1)
    upper_edge = from_behind(whole[:, :1], "blk", -1)
    below = jnp.concatenate([lower_edge, whole[:, :-1]], axis=1)
    above = jnp.concatenate([whole[:, 1:], upper_edge], axis=1)
    partial_value = jnp.zeros_like(whole)
    for term_idx in range(left_env.shape[0]):
        charge = term_charge[term_idx]
        source = jnp.where(charge == 1, below, jnp.where(charge == -1, above, whole))
        mixed = jnp.einsum("pq,qiab->piab", local_mpo[term_idx], source, precision=HI)
        inner = jnp.einsum("iac,picb->piab", left_env[term_idx], mixed, precision=HI)
        partial_value = partial_value + jnp.einsum(
            "piac,ibc->piab", inner, right_env[term_idx], precision=HI
        )
    summed = lax.psum_scatter(partial_value, "term", scatter_dimension=2, tiled=True)
    return summed * row_mask


def per_device(start_vec, left_env, right_env, local_mpo, term_charge, sector_sizes, sector_ranks):
    width = start_vec.shape[3]
    row_count = start_vec.shape[2]
    states = start_vec.shape[0]
    sectors = start_vec.shape[1] * lax.axis_size("blk")
    row_start = lax.axis_index("term") * row_count
    row_ids = row_start + jnp.arange(row_count, dtype=jnp.int32)
    col_live = live_mask(sector_sizes, width)
    row_live = (row_ids[None, :] < sector_sizes[:, None]).astype(jnp.float32)
    row_mask = (row_live[:, :, None] * col_live[:, None, :])[None]
    start = start_vec * row_mask
    start_sq = lax.psum(jnp.sum(start * start), ("term", "blk"))
    vector = start / jnp.sqrt(start_sq + 1e-06)
    previous = jnp.zeros_like(vector)
    beta = jnp.float32(0.0)
    alphas = []
    betas = []
    for step in range(KRY):
        image = apply_operator(vector, left_env, right_env, local_mpo, term_charge, row_mask)
        alpha = lax.psum(jnp.sum(vector * image), ("term", "blk"))
        resid = image - alpha * vector - beta * previous
        norm_sq = lax.psum(jnp.sum(resid * resid), ("term", "blk"))
        new_beta = jnp.sqrt(norm_sq + 1e-06)
        previous = vector
        vector = resid / new_beta
        beta = new_beta
        alphas.append(alpha)
        betas.append(new_beta)
    coeffs = jnp.stack([jnp.stack(alphas), jnp.stack(betas)])
    krylov = jnp.sqrt(jnp.float32(sectors * states)) * width * vector
    whole = lax.all_gather(vector, "term", axis=2, tiled=True)
    gram = jnp.einsum("piab,picb->iac", vector, whole, precision=HI)
    kept_rows = (row_ids[None, :] < sector_ranks[:, None]).astype(jnp.float32)
    kept_cols = live_mask(sector_ranks, width)
    density = sectors * width * gram * kept_rows[:, :, None] * kept_cols[:, None, :]
    return (coeffs, krylov, density)


def solution(mesh):
    placed = (
        P(None, "blk", "term", None),
        P("term", "blk", None, None),
        P("term", "blk", None, None),
        P("term", None, None),
        P("term"),
        P("blk"),
        P("blk"),
    )
    return jax.shard_map(
        per_device,
        mesh=mesh,
        in_specs=placed,
        out_specs=(P(), P(None, "blk", "term", None), P("blk", "term", None)),
        check_vma=False,
    )
```

profile of v0, /device:TPU:1, one launch (start us, length us, event | category | flops | bytes accessed | tf_op | source)
XLA Modules:
  0.0 1138.8 jit_solution(13823765751288833090)
XLA Ops:
  9.7 41.0 %psum.119 = f32[]{:T(128)} all-reduce(f32[]{:T(128)} %multiply_reduce_fusion.16), channel_id=1, replica_groups=mesh['term'=2,'blk'=16] {'term','blk'}, use_global_device_ids=true, to_apply=%region_1.0 | all-reduce | flops 1 | bytes 8 | tf_op jit(solution)/shard_map/psum | solution.py:52
  51.4 6.7 all_gather.27
  58.2 4.6 collective-permute-start.1
  62.7 2.9 collective-permute-start
  87.0 13.3 %reduce-scatter.9.cloned.1.call-done = f32[4,2,64,128]{3,2,0,1:T(8,128)} async-done(((f32[4,2,128,128]{3,2,0,1:T(8,128)}), f32[4,2,64,128]{3,2,0,1:T(8,128)}) %reduce-scatter.9.cloned.1.call-update) | async-done | bytes 262160 | tf_op jit(solution)/shard_map/reduce_scatter | solution.py:37
  102.0 38.9 %psum.120 = f32[]{:T(128)} all-reduce(f32[]{:T(128)} %multiply_reduce_fusion.15), channel_id=1, replica_groups=mesh['term'=2,'blk'=16] {'term','blk'}, use_global_device_ids=true, to_apply=%region_4.5 | all-reduce | flops 1 | bytes 8 | tf_op jit(solution)/shard_map/psum | solution.py:60
  142.3 41.5 %psum.121 = f32[]{:T(128)} all-reduce(f32[]{:T(128)} %multiply_reduce_fusion.14), channel_id=1, replica_groups=mesh['term'=2,'blk'=16] {'term','blk'}, use_global_device_ids=true, to_apply=%region_6.7 | all-reduce | flops 1 | bytes 8 | tf_op jit(solution)/shard_map/psum | solution.py:62
  185.2 6.7 all_gather.28
  192.0 4.6 collective-permute-start.3
  214.4 11.8 %convolution_add_fusion.19 = f32[2,4,128,128]{3,2,1,0:T(8,128)S(1)} fusion(f32[2,4,128,128]{3,2,1,0:T(8,128)S(1)} %convolution_add_fusion.20, f32[4,2,128,128]{2,3,0,1:T(8,128)S(1)} %convolution_bitcast_fusion.50, f32[4,2,128,128]{3,2,1,0:T(8,128)S(1)} %copy-done.1), kind=kOutput, calls=%fused_computation.90 | convolution fusion | flops 201457664 | bytes 1703936 | tf_op jit(solution)/shard_map/piac,ibc->piab/dot_general | solution.py:34
  228.1 15.2 %reduce-scatter.11.cloned.1.call-done = f32[4,2,64,128]{3,2,0,1:T(8,128)} async-done(((f32[4,2,128,128]{3,2,0,1:T(8,128)}), f32[4,2,64,128]{3,2,0,1:T(8,128)}) %reduce-scatter.11.cloned.1.call-update) | async-done | bytes 262160 | tf_op jit(solution)/shard_map/reduce_scatter | solution.py:37
  245.0 38.8 %psum.122 = f32[]{:T(128)} all-reduce(f32[]{:T(128)} %multiply_reduce_fusion.13), channel_id=1, replica_groups=mesh['term'=2,'blk'=16] {'term','blk'}, use_global_device_ids=true, to_apply=%region_9.10 | all-reduce | flops 1 | bytes 8 | tf_op jit(solution)/shard_map/psum | solution.py:60
  285.1 41.4 %psum.123 = f32[]{:T(128)} all-reduce(f32[]{:T(128)} %get-tuple-element.26), channel_id=1, replica_groups=mesh['term'=2,'blk'=16] {'term','blk'}, use_global_device_ids=true, to_apply=%region_11.12 | all-reduce | flops 1 | bytes 8 | tf_op jit(solution)/shard_map/psum | solution.py:62
  327.2 6.7 all_gather.29
  334.0 4.6 collective-permute-start.5
  359.6 15.2 %reduce-scatter.13.cloned.1.call-done = f32[4,2,64,128]{3,2,0,1:T(8,128)} async-done(((f32[4,2,128,128]{3,2,0,1:T(8,128)}), f32[4,2,64,128]{3,2,0,1:T(8,128)}) %reduce-scatter.13.cloned.1.call-update) | async-done | bytes 262160 | tf_op jit(solution)/shard_map/reduce_scatter | solution.py:37
  376.6 38.8 %psum.124 = f32[]{:T(128)} all-reduce(f32[]{:T(128)} %multiply_reduce_fusion.11), channel_id=1, replica_groups=mesh['term'=2,'blk'=16] {'term','blk'}, use_global_device_ids=true, to_apply=%region_14.15 | all-reduce | flops 1 | bytes 8 | tf_op jit(solution)/shard_map/psum | solution.py:60
  416.7 41.4 %psum.125 = f32[]{:T(128)} all-reduce(f32[]{:T(128)} %get-tuple-element.24), channel_id=1, replica_groups=mesh['term'=2,'blk'=16] {'term','blk'}, use_global_device_ids=true, to_apply=%region_16.17 | all-reduce | flops 1 | bytes 8 | tf_op jit(solution)/shard_map/psum | solution.py:62
  458.8 6.7 all_gather.30
  465.5 4.6 collective-permute-start.7
  470.1 2.9 collective-permute-start.6
  491.0 15.2 %reduce-scatter.15.cloned.1.call-done = f32[4,2,64,128]{3,2,0,1:T(8,128)} async-done(((f32[4,2,128,128]{3,2,0,1:T(8,128)}), f32[4,2,64,128]{3,2,0,1:T(8,128)}) %reduce-scatter.15.cloned.1.call-update) | async-done | bytes 262160 | tf_op jit(solution)/shard_map/reduce_scatter | solution.py:37
  508.0 39.0 %psum.126 = f32[]{:T(128)} all-reduce(f32[]{:T(128)} %multiply_reduce_fusion.9), channel_id=1, replica_groups=mesh['term'=2,'blk'=16] {'term','blk'}, use_global_device_ids=true, to_apply=%region_19.20 | all-reduce | flops 1 | bytes 8 | tf_op jit(solution)/shard_map/psum | solution.py:60
  548.4 41.4 %psum.127 = f32[]{:T(128)} all-reduce(f32[]{:T(128)} %get-tuple-element.22), channel_id=1, replica_groups=mesh['term'=2,'blk'=16] {'term','blk'}, use_global_device_ids=true, to_apply=%region_21.22 | all-reduce | flops 1 | bytes 8 | tf_op jit(solution)/shard_map/psum | solution.py:62
  590.5 6.7 all_gather.31
  597.3 4.6 collective-permute-start.9
  622.9 15.3 %reduce-scatter.17.cloned.1.call-done = f32[4,2,64,128]{3,2,0,1:T(8,128)} async-done(((f32[4,2,128,128]{3,2,0,1:T(8,128)}), f32[4,2,64,128]{3,2,0,1:T(8,128)}) %reduce-scatter.17.cloned.1.call-update) | async-done | bytes 262160 | tf_op jit(solution)/shard_map/reduce_scatter | solution.py:37
  640.0 39.0 %psum.128 = f32[]{:T(128)} all-reduce(f32[]{:T(128)} %multiply_reduce_fusion.7), channel_id=1, replica_groups=mesh['term'=2,'blk'=16] {'term','blk'}, use_global_device_ids=true, to_apply=%region_24.25 | all-reduce | flops 1 | bytes 8 | tf_op jit(solution)/shard_map/psum | solution.py:60
  680.4 41.4 %psum.129 = f32[]{:T(128)} all-reduce(f32[]{:T(128)} %get-tuple-element.20), channel_id=1, replica_groups=mesh['term'=2,'blk'=16] {'term','blk'}, use_global_device_ids=true, to_apply=%region_26.27 | all-reduce | flops 1 | bytes 8 | tf_op jit(solution)/shard_map/psum | solution.py:62
  722.4 6.7 all_gather.32
  729.2 4.6 collective-permute-start.11
  733.8 2.9 collective-permute-start.10
  754.7 15.2 %reduce-scatter.19.cloned.1.call-done = f32[4,2,64,128]{3,2,0,1:T(8,128)} async-done(((f32[4,2,128,128]{3,2,0,1:T(8,128)}), f32[4,2,64,128]{3,2,0,1:T(8,128)}) %reduce-scatter.19.cloned.1.call-update) | async-done | bytes 262160 | tf_op jit(solution)/shard_map/reduce_scatter | solution.py:37
  771.6 38.8 %psum.130 = f32[]{:T(128)} all-reduce(f32[]{:T(128)} %multiply_reduce_fusion.5), channel_id=1, replica_groups=mesh['term'=2,'blk'=16] {'term','blk'}, use_global_device_ids=true, to_apply=%region_29.30 | all-reduce | flops 1 | bytes 8 | tf_op jit(solution)/shard_map/psum | solution.py:60
  811.8 41.4 %psum.131 = f32[]{:T(128)} all-reduce(f32[]{:T(128)} %get-tuple-element.18), channel_id=1, replica_groups=mesh['term'=2,'blk'=16] {'term','blk'}, use_global_device_ids=true, to_apply=%region_31.32 | all-reduce | flops 1 | bytes 8 | tf_op jit(solution)/shard_map/psum | solution.py:62
  853.8 6.7 all_gather.33
  860.6 4.6 collective-permute-start.13
  886.0 15.2 %reduce-scatter.21.cloned.1.call-done = f32[4,2,64,128]{3,2,0,1:T(8,128)} async-done(((f32[4,2,128,128]{3,2,0,1:T(8,128)}), f32[4,2,64,128]{3,2,0,1:T(8,128)}) %reduce-scatter.21.cloned.1.call-update) | async-done | bytes 262160 | tf_op jit(solution)/shard_map/reduce_scatter | solution.py:37
  903.0 38.9 %psum.132 = f32[]{:T(128)} all-reduce(f32[]{:T(128)} %multiply_reduce_fusion.3), channel_id=1, replica_groups=mesh['term'=2,'blk'=16] {'term','blk'}, use_global_device_ids=true, to_apply=%region_34.35 | all-reduce | flops 1 | bytes 8 | tf_op jit(solution)/shard_map/psum | solution.py:60
  943.3 41.4 %psum.133 = f32[]{:T(128)} all-reduce(f32[]{:T(128)} %get-tuple-element.16), channel_id=1, replica_groups=mesh['term'=2,'blk'=16] {'term','blk'}, use_global_device_ids=true, to_apply=%region_36.37 | all-reduce | flops 1 | bytes 8 | tf_op jit(solution)/shard_map/psum | solution.py:62
  985.3 6.7 all_gather.34
  992.1 4.6 collective-permute-start.15
  996.7 2.9 collective-permute-start.14
  1018.3 14.6 %reduce-scatter.23.cloned.1.call-done = f32[4,2,64,128]{3,2,0,1:T(8,128)} async-done(((f32[4,2,128,128]{3,2,0,1:T(8,128)}), f32[4,2,64,128]{3,2,0,1:T(8,128)}) %reduce-scatter.23.cloned.1.call-update) | async-done | bytes 262160 | tf_op jit(solution)/shard_map/reduce_scatter | solution.py:37
  1034.7 38.9 %psum.134 = f32[]{:T(128)} all-reduce(f32[]{:T(128)} %multiply_reduce_fusion.1), channel_id=1, replica_groups=mesh['term'=2,'blk'=16] {'term','blk'}, use_global_device_ids=true, to_apply=%region_39.40 | all-reduce | flops 1 | bytes 8 | tf_op jit(solution)/shard_map/psum | solution.py:60
  1074.9 41.4 %psum.135 = f32[]{:T(128)} all-reduce(f32[]{:T(128)} %get-tuple-element.14), channel_id=1, replica_groups=mesh['term'=2,'blk'=16] {'term','blk'}, use_global_device_ids=true, to_apply=%region_41.42 | all-reduce | flops 1 | bytes 8 | tf_op jit(solution)/shard_map/psum | solution.py:62
  1117.8 6.7 all_gather.35
  1124.6 5.1 stack.71
  (222 shorter events, 183.8 us)
Async XLA Ops:
  7.2 0.7 copy-start.13
  7.2 44.2 %copy-start.2 = (f32[4,2,64,128]{3,2,1,0:T(8,128)S(1)}, f32[4,2,64,128]{3,2,1,0:T(8,128)}, u32[]{:S(2)}) copy-start(f32[4,2,64,128]{3,2,1,0:T(8,128)} %param.7) | copy-start | bytes 786436
  7.2 93.1 %reduce-scatter.9.cloned.1.call-start = ((), (), s32[]{:S(2)}) async-start(), calls=%async_computation.8 | async-start | bytes 786432 | tf_op jit(solution)/shard_map/reduce_scatter | solution.py:37
  58.2 7.5 copy-start.12
  58.2 13.4 %collective-permute-start.1 = (f32[4,1,128,128]{3,2,0,1:T(8,128)S(1)}, f32[4,1,128,128]{3,2,0,1:T(8,128)S(1)}, u32[]{:S(2)}, u32[]{:S(2)}) collective-permute-start(f32[4,1,128,128]{3,2,0,1:T(8,128)S(1)} %get-tuple-element.67), channel_id=1, source_target_pairs={{1,0},{2,1},{3,2},{4,3},{5,4},{6,5},{7,6},{8,7},{9,8},{10,9},{11,1... | collective-permute-start | bytes 786440 | tf_op jit(solution)/shard_map/ppermute | solution.py:15
  62.7 8.9 collective-permute-start
  71.6 0.7 copy-start.11
  73.8 1.3 copy-start
  80.8 1.0 copy-start.1
  86.9 156.5 %reduce-scatter.11.cloned.1.call-start = ((), (), s32[]{:S(2)}) async-start(), calls=%async_computation.9 | async-start | bytes 786432 | tf_op jit(solution)/shard_map/reduce_scatter | solution.py:37
  100.3 40.6 %copy-start.3 = (f32[4,2,64,128]{3,2,0,1:T(8,128)S(1)}, f32[4,2,64,128]{3,2,0,1:T(8,128)}, u32[]{:S(2)}) copy-start(f32[4,2,64,128]{3,2,0,1:T(8,128)} %reduce-scatter.9.cloned.1.call-done) | copy-start | bytes 786436
  192.0 9.6 collective-permute-start.3
  196.6 6.3 collective-permute-start.2
  228.1 146.8 %reduce-scatter.13.cloned.1.call-start = ((), (), s32[]{:S(2)}) async-start(), calls=%async_computation.10 | async-start | bytes 786432 | tf_op jit(solution)/shard_map/reduce_scatter | solution.py:37
  243.4 40.5 %copy-start.10 = (f32[4,2,64,128]{3,2,0,1:T(8,128)S(1)}, f32[4,2,64,128]{3,2,0,1:T(8,128)}, u32[]{:S(2)}) copy-start(f32[4,2,64,128]{3,2,0,1:T(8,128)} %reduce-scatter.11.cloned.1.call-done) | copy-start | bytes 786436
  334.0 9.5 collective-permute-start.5
  338.6 6.2 collective-permute-start.4
  359.6 146.7 %reduce-scatter.15.cloned.1.call-start = ((), (), s32[]{:S(2)}) async-start(), calls=%async_computation.11 | async-start | bytes 786432 | tf_op jit(solution)/shard_map/reduce_scatter | solution.py:37
  374.9 40.5 %copy-start.5 = (f32[4,2,64,128]{3,2,0,1:T(8,128)S(1)}, f32[4,2,64,128]{3,2,0,1:T(8,128)}, u32[]{:S(2)}) copy-start(f32[4,2,64,128]{3,2,0,1:T(8,128)} %reduce-scatter.13.cloned.1.call-done) | copy-start | bytes 786436
  465.5 9.6 collective-permute-start.7
  470.1 6.3 collective-permute-start.6
  490.9 147.3 %reduce-scatter.17.cloned.1.call-start = ((), (), s32[]{:S(2)}) async-start(), calls=%async_computation.12 | async-start | bytes 786432 | tf_op jit(solution)/shard_map/reduce_scatter | solution.py:37
  506.2 40.8 %copy-start.6 = (f32[4,2,64,128]{3,2,0,1:T(8,128)S(1)}, f32[4,2,64,128]{3,2,0,1:T(8,128)}, u32[]{:S(2)}) copy-start(f32[4,2,64,128]{3,2,0,1:T(8,128)} %reduce-scatter.15.cloned.1.call-done) | copy-start | bytes 786436
  597.3 9.5 collective-permute-start.9
  601.9 6.2 collective-permute-start.8
  622.9 147.0 %reduce-scatter.19.cloned.1.call-start = ((), (), s32[]{:S(2)}) async-start(), calls=%async_computation.13 | async-start | bytes 786432 | tf_op jit(solution)/shard_map/reduce_scatter | solution.py:37
  638.2 40.8 %copy-start.7 = (f32[4,2,64,128]{3,2,0,1:T(8,128)S(1)}, f32[4,2,64,128]{3,2,0,1:T(8,128)}, u32[]{:S(2)}) copy-start(f32[4,2,64,128]{3,2,0,1:T(8,128)} %reduce-scatter.17.cloned.1.call-done) | copy-start | bytes 786436
  729.2 9.6 collective-permute-start.11
  733.8 6.3 collective-permute-start.10
  754.6 146.7 %reduce-scatter.21.cloned.1.call-start = ((), (), s32[]{:S(2)}) async-start(), calls=%async_computation.14 | async-start | bytes 786432 | tf_op jit(solution)/shard_map/reduce_scatter | solution.py:37
  769.9 40.5 %copy-start.8 = (f32[4,2,64,128]{3,2,0,1:T(8,128)S(1)}, f32[4,2,64,128]{3,2,0,1:T(8,128)}, u32[]{:S(2)}) copy-start(f32[4,2,64,128]{3,2,0,1:T(8,128)} %reduce-scatter.19.cloned.1.call-done) | copy-start | bytes 786436
  860.6 9.5 collective-permute-start.13
  865.2 6.2 collective-permute-start.12
  886.0 146.9 %reduce-scatter.23.cloned.1.call-start = ((), (), s32[]{:S(2)}) async-start(), calls=%async_computation.15 | async-start | bytes 786432 | tf_op jit(solution)/shard_map/reduce_scatter | solution.py:37
  901.3 40.6 %copy-start.9 = (f32[4,2,64,128]{3,2,0,1:T(8,128)S(1)}, f32[4,2,64,128]{3,2,0,1:T(8,128)}, u32[]{:S(2)}) copy-start(f32[4,2,64,128]{3,2,0,1:T(8,128)} %reduce-scatter.21.cloned.1.call-done) | copy-start | bytes 786436
  992.1 9.6 collective-permute-start.15
  996.7 6.3 collective-permute-start.14
  1017.6 0.7 copy-start.14
  1032.9 40.6 %copy-start.4 = (f32[4,2,64,128]{3,2,0,1:T(8,128)S(1)}, f32[4,2,64,128]{3,2,0,1:T(8,128)}, u32[]{:S(2)}) copy-start(f32[4,2,64,128]{3,2,0,1:T(8,128)} %reduce-scatter.23.cloned.1.call-done) | copy-start | bytes 786436
Sparse Core Ops, SparseCore 0:
  87.0 13.2 reduce-scatter.8
  228.2 15.1 reduce-scatter.10
  359.7 15.1 reduce-scatter.12
  491.1 15.1 reduce-scatter.14
  623.0 15.1 reduce-scatter.16
  754.7 15.1 reduce-scatter.18
  886.1 15.1 reduce-scatter.20
  1017.7 15.1 reduce-scatter.22
where the time goes:
time: 1150 us; the launch traced here: 1140 us
  blocking collectives  744 us (65%)
  waiting for transfers between devices  143 us (12%)
  matrix products  126 us (11%)
  starting transfers between devices  59.7 us (5%)
  other arithmetic  30.5 us (3%)
  between operations  26.6 us (2%)
    psum x8, blocking collectives, per_device(): norm_sq = lax.psum(jnp.sum(resid * resid), ('term', 'blk'))  331 us
    psum x8, blocking collectives, per_device(): alpha = lax.psum(jnp.sum(vector * image), ('term', 'blk'))  311 us
    reduce_scatter x8, waiting for transfers between devices, apply_operator(): lax.psum_scatter(partial_value, 'term', scatter_dimension=2, tiled=True)  119 us
    ppermute x16, starting transfers between devices, from_behind(): return lax.ppermute(value, axis, pairs)  59.3 us
    all_gather x8, blocking collectives, apply_operator(): whole = lax.all_gather(rows_vec, 'term', axis=2, tiled=True)  53.9 us
    dot_general x32, matrix products, apply_operator(): jnp.einsum('piac,ibc->piab', inner, right_env[term_idx], precision=HI)  51 us
    dot_general x32, matrix products, apply_operator(): jnp.einsum('pq,qiab->piab', local_mpo[term_idx], source, precision=HI)  41.9 us
    psum x1, blocking collectives, per_device(): start_sq = lax.psum(jnp.sum(start * start), ('term', 'blk'))  41 us
  transfers between devices with their start and end apart: 24, of which 22 were waited for; matrix products, arithmetic and copies ran while one was open for 0% of the time, Pallas kernels for 0%

commit v1 on v0

--- a/solution.py
+++ b/solution.py
@@ -2,6 +2,8 @@
 import jax.numpy as jnp
 from jax import lax
 from jax.sharding import PartitionSpec as P
+from jax.experimental import pallas as pl
+from jax.experimental.pallas import tpu as pltpu
 
 KRY = 8
 
@@ -76,7 +78,481 @@
     return (coeffs, krylov, density)
 
 
+MESH = pl.DeviceIdType.MESH
+BF = jnp.bfloat16
+F32 = jnp.float32
+
+
+def split(value):
+    high = value.astype(BF)
+    low = (value - high.astype(F32)).astype(BF)
+    return high, low
+
+
+def mm(left, right):
+    return jnp.dot(left, right, preferred_element_type=F32)
+
+
+def mm_t(left, right):
+    return lax.dot_general(left, right, (((1,), (1,)), ((), ())), preferred_element_type=F32)
+
+
+def lanczos_kernel(
+    groups,
+    start_ref, left_ref, right_ref, meta_ref, sizes_ref, ranks_ref,
+    coeffs_ref, krylov_ref, density_ref,
+    x_send, l_send, r_send, x_got, l_got, r_got, meta_got,
+    images, vectors, below, above,
+    l_split, r_split, mixed, applied,
+    pair_sums, all_sums, marks, out_send, den_send, den_got,
+    init_send, init_recv, meta_send, meta_recv,
+    halo_send, halo_recv, pair_send, pair_recv, all_send, all_recv,
+    out_ssem, out_rsem,
+):
+    states, _, rows, width = start_ref.shape
+    terms = left_ref.shape[0]
+    t = lax.axis_index("term")
+    b = lax.axis_index("blk")
+    k = b // 2
+    c = b % 2
+    flip = k % 2
+    me = t * 2 + c
+    half = (t + flip) % 2
+    part = (c + half) % 2
+    sector = 4 * k + 2 * half + part
+    has_lower = sector > 0
+    has_upper = sector < 4 * groups - 1
+
+    def owner(index):
+        group = index // 4
+        rest = index % 4
+        own_half = rest // 2
+        own_part = rest % 2
+        return ((own_half + group) % 2, group * 2 + (own_part + own_half) % 2)
+
+    lower_dev = owner(jnp.maximum(sector - 1, 0))
+    upper_dev = owner(jnp.minimum(sector + 1, 4 * groups - 1))
+
+    def pair_dev(step):
+        other = (me + step) % 4
+        return other, (other // 2, k * 2 + other % 2)
+
+    def group_dev(step):
+        other = (k + step) % groups
+        return other, (t, other * 2 + c)
+
+    below[...] = jnp.zeros_like(below)
+    above[...] = jnp.zeros_like(above)
+    images[...] = jnp.zeros_like(images)
+    vectors[...] = jnp.zeros_like(vectors)
+
+    barrier = pltpu.get_barrier_semaphore()
+    for step in range(1, 4):
+        pl.semaphore_signal(barrier, inc=1, device_id=pair_dev(step)[1], device_id_type=MESH)
+    for step in range(1, groups):
+        pl.semaphore_signal(barrier, inc=1, device_id=group_dev(step)[1], device_id_type=MESH)
+
+    row_ids = lax.broadcasted_iota(jnp.int32, (width, width), 0)
+    col_ids = lax.broadcasted_iota(jnp.int32, (rows, width), 1)
+    sub_ids = lax.broadcasted_iota(jnp.int32, (rows, width), 0) + t * rows
+    for s in range(2):
+        size = sizes_ref[s]
+        live = (sub_ids < size) & (col_ids < size)
+        for p in range(states):
+            x_send[s, p] = jnp.where(live, start_ref[p, s], 0.0)
+        for w in range(terms):
+            l_send[s, w] = jnp.where(row_ids < size, left_ref[w, s], 0.0)
+            r_send[s, w] = jnp.where(row_ids < size, right_ref[w, s], 0.0)
+
+    pl.semaphore_wait(barrier, 3 + groups - 1)
+
+    pieces = ((x_send, x_got), (l_send, l_got), (r_send, r_got))
+    target_t = (c + flip) % 2
+
+    def init_copy(s, j):
+        src, dst = pieces[j]
+        return pltpu.make_async_remote_copy(
+            src_ref=src.at[s], dst_ref=dst.at[t],
+            send_sem=init_send.at[s, j], recv_sem=init_recv.at[t, j],
+            device_id=(target_t, k * 2 + (s + c) % 2), device_id_type=MESH,
+        )
+
+    keeps = target_t == t
+    partner = pair_dev(2)[1]
+    meta_copy = pltpu.make_async_remote_copy(
+        src_ref=meta_ref, dst_ref=meta_got.at[t],
+        send_sem=meta_send, recv_sem=meta_recv,
+        device_id=partner, device_id_type=MESH,
+    )
+    for j in range(3):
+        @pl.when(jnp.logical_not(keeps))
+        def _():
+            init_copy(0, j).start()
+        init_copy(1, j).start()
+        if j == 0:
+            meta_copy.start()
+
+    @pl.when(keeps)
+    def _():
+        x_got[t] = x_send[0]
+        l_got[t] = l_send[0]
+        r_got[t] = r_send[0]
+
+    meta_got[t] = meta_ref[...]
+
+    def init_wait(source, j):
+        src, dst = pieces[j]
+        @pl.when(jnp.logical_not((source == t) & (half == c)))
+        def _():
+            pltpu.make_async_remote_copy(
+                src_ref=src.at[0], dst_ref=dst.at[source],
+                send_sem=init_send.at[0, j], recv_sem=init_recv.at[source, j],
+                device_id=partner, device_id_type=MESH,
+            ).wait_recv()
+
+    for source in range(2):
+        init_wait(source, 0)
+        images[0, :, pl.ds(source * rows, rows), :] = x_got[source]
+
+    def lane_sums(first, second):
+        total = first[0] * second[0]
+        for p in range(1, states):
+            total = total + first[p] * second[p]
+        return jnp.sum(total, axis=0, keepdims=True)
+
+    def write_products(slot, image, vector, before):
+        pair_sums[slot, me] = jnp.concatenate(
+            [
+                lane_sums(image, image), lane_sums(vector, image), lane_sums(before, image),
+                lane_sums(vector, vector), lane_sums(before, vector), lane_sums(before, before),
+                jnp.zeros((2, width), F32),
+            ],
+            axis=0,
+        )
+
+    def pair_copy(slot, step):
+        return pltpu.make_async_remote_copy(
+            src_ref=pair_sums.at[slot, me], dst_ref=pair_sums.at[slot, me],
+            send_sem=pair_send.at[step - 1], recv_sem=pair_recv.at[slot, me],
+            device_id=pair_dev(step)[1], device_id_type=MESH,
+        )
+
+    def group_copy(slot, step):
+        return pltpu.make_async_remote_copy(
+            src_ref=all_sums.at[slot, k], dst_ref=all_sums.at[slot, k],
+            send_sem=all_send.at[step - 1], recv_sem=all_recv.at[slot, k],
+            device_id=group_dev(step)[1], device_id_type=MESH,
+        )
+
+    def start_pair(slot):
+        for step in range(1, 4):
+            pair_copy(slot, step).start()
+
+    def finish_pair(slot):
+        for step in range(1, 4):
+            other, dev = pair_dev(step)
+            pltpu.make_async_remote_copy(
+                src_ref=pair_sums.at[slot, me], dst_ref=pair_sums.at[slot, other],
+                send_sem=pair_send.at[step - 1], recv_sem=pair_recv.at[slot, other],
+                device_id=dev, device_id_type=MESH,
+            ).wait_recv()
+        total = pair_sums[slot, 0]
+        for other in range(1, 4):
+            total = total + pair_sums[slot, other]
+        all_sums[slot, k] = total
+        for step in range(1, groups):
+            group_copy(slot, step).start()
+
+    def finish_sums(slot, beta_before):
+        for step in range(1, groups):
+            other, dev = group_dev(step)
+            pltpu.make_async_remote_copy(
+                src_ref=all_sums.at[slot, k], dst_ref=all_sums.at[slot, other],
+                send_sem=all_send.at[step - 1], recv_sem=all_recv.at[slot, other],
+                device_id=dev, device_id_type=MESH,
+            ).wait_recv()
+        total = all_sums[slot, 0]
+        for other in range(1, groups):
+            total = total + all_sums[slot, other]
+        dots = jnp.sum(total, axis=1, keepdims=True)
+        ww, vw, uw, vv, uv, uu = (dots[i:i + 1] for i in range(6))
+        alpha = vw
+        norm_sq = (
+            ww - 2.0 * alpha * vw - 2.0 * beta_before * uw
+            + alpha * alpha * vv + beta_before * beta_before * uu
+            + 2.0 * alpha * beta_before * uv
+        )
+        beta = jnp.sqrt(jnp.maximum(norm_sq, 0.0) + 1e-06)
+        for step in range(1, 4):
+            pair_copy(slot, step).wait_send()
+        for step in range(1, groups):
+            group_copy(slot, step).wait_send()
+        return alpha, beta
+
+    def down_copy(slot):
+        return pltpu.make_async_remote_copy(
+            src_ref=images.at[slot], dst_ref=above.at[slot],
+            send_sem=halo_send.at[0], recv_sem=halo_recv.at[slot, 0],
+            device_id=lower_dev, device_id_type=MESH,
+        )
+
+    def up_copy(slot):
+        return pltpu.make_async_remote_copy(
+            src_ref=images.at[slot], dst_ref=below.at[slot],
+            send_sem=halo_send.at[1], recv_sem=halo_recv.at[slot, 1],
+            device_id=upper_dev, device_id_type=MESH,
+        )
+
+    def start_halo(slot):
+        @pl.when(has_lower)
+        def _():
+            down_copy(slot).start()
+
+        @pl.when(has_upper)
+        def _():
+            up_copy(slot).start()
+
+    def wait_halo(slot):
+        @pl.when(has_lower)
+        def _():
+            up_copy(slot).wait_recv()
+
+        @pl.when(has_upper)
+        def _():
+            down_copy(slot).wait_recv()
+
+    def wait_halo_send(slot):
+        @pl.when(has_lower)
+        def _():
+            down_copy(slot).wait_send()
+
+        @pl.when(has_upper)
+        def _():
+            up_copy(slot).wait_send()
+
+    start_halo(0)
+    first = images[0]
+    write_products(0, first, vectors[0], vectors[1])
+    start_pair(0)
+
+    meta_copy.wait_recv()
+    for source in range(2):
+        init_wait(source, 1)
+        for w in range(terms):
+            high, low = split(l_got[source, w])
+            l_split[source * terms + w] = jnp.concatenate([high, low], axis=1)
+    for source in range(2):
+        init_wait(source, 2)
+        for w in range(terms):
+            high, low = split(r_got[source, w].T)
+            r_split[pl.ds((source * terms + w) * width, width), :] = jnp.concatenate([high, low], axis=1)
+
+    def apply(slot):
+        for w in range(2 * terms):
+            source, local = w // terms, w % terms
+            charge = meta_got[source, pl.ds(states * states * terms + local, 1), :]
+            from_below = charge > 0.5
+            from_above = charge < -0.5
+            vec = jnp.concatenate(
+                [
+                    jnp.where(from_below, below[slot, q], jnp.where(from_above, above[slot, q], images[slot, q]))
+                    for q in range(states)
+                ],
+                axis=1,
+            )
+            high, low = split(vec)
+            both = l_split[w]
+            inner = mm(both, jnp.concatenate([high, high], axis=0)) + mm(both[:, :width], low)
+            for p in range(states):
+                total = None
+                for q in range(states):
+                    row = local * states * states + p * states + q
+                    factor = meta_got[source, pl.ds(row, 1), :]
+                    piece = factor * inner[:, q * width:(q + 1) * width]
+                    total = piece if total is None else total + piece
+                high, low = split(total)
+                mixed[pl.ds(p * width, width), pl.ds(w * width, width)] = high
+                mixed[pl.ds((states + p) * width, width), pl.ds(w * width, width)] = low
+        stacked = states * width
+        top = mm(mixed[pl.ds(0, stacked), :], r_split[...])
+        bottom = mm(mixed[pl.ds(stacked, stacked), :], r_split[:, :width])
+        applied[...] = top[:, :width] + top[:, width:] + bottom
+
+    lanes = lax.broadcasted_iota(jnp.int32, marks.shape, 1)
+    subs = lax.broadcasted_iota(jnp.int32, marks.shape, 0)
+    marks[...] = jnp.zeros_like(marks)
+
+    def record(index, alpha, beta):
+        here = lanes == index
+        marks[...] = jnp.where(here & (subs == 0), alpha, jnp.where(here & (subs == 1), beta, marks[...]))
+
+    def step_body(it, beta_before):
+        slot = it % 2
+        other = 1 - slot
+        wait_halo(slot)
+        finish_pair(slot)
+        apply(slot)
+        alpha, beta = finish_sums(slot, beta_before)
+        record(it - 1, alpha, beta)
+        scale = 1.0 / beta
+        for p in range(states):
+            image = images[slot, p]
+            vector = vectors[slot, p]
+            done = applied[pl.ds(p * width, width), :]
+            vectors[other, p] = (image - alpha * vector - beta_before * vectors[other, p]) * scale
+            images[other, p] = (done - alpha * image - beta_before * images[other, p]) * scale
+        wait_halo_send(slot)
+
+        @pl.when(it < KRY - 1)
+        def _():
+            start_halo(other)
+
+        write_products(other, images[other], vectors[other], vectors[slot])
+        start_pair(other)
+        return jnp.where(it == 0, 0.0, beta)
+
+    beta_before = lax.fori_loop(0, KRY, step_body, jnp.zeros((1, 1), F32))
+    slot = KRY % 2
+    finish_pair(slot)
+    alpha, beta = finish_sums(slot, beta_before)
+    record(KRY - 1, alpha, beta)
+    coeffs_ref[...] = marks[:2, :KRY]
+    scale = 1.0 / beta
+    last = [
+        (images[slot, p] - alpha * vectors[slot, p] - beta_before * vectors[1 - slot, p]) * scale
+        for p in range(states)
+    ]
+    sectors = 4 * groups
+    stretch = float((sectors * states) ** 0.5) * width
+    for p in range(states):
+        for r in range(2):
+            out_send[r, p] = stretch * last[p][r * rows:(r + 1) * rows]
+
+    def krylov_copy(r):
+        return pltpu.make_async_remote_copy(
+            src_ref=out_send.at[r], dst_ref=krylov_ref.at[:, part],
+            send_sem=out_ssem.at[0, r], recv_sem=out_rsem.at[0, part],
+            device_id=(r, k * 2 + half), device_id_type=MESH,
+        )
+
+    def density_copy(r):
+        return pltpu.make_async_remote_copy(
+            src_ref=den_send.at[r], dst_ref=den_got.at[part],
+            send_sem=out_ssem.at[1, r], recv_sem=out_rsem.at[1, part],
+            device_id=(r, k * 2 + half), device_id_type=MESH,
+        )
+
+    def is_self(r):
+        return (t == r) & (half == c)
+
+    for r in range(2):
+        @pl.when(jnp.logical_not(is_self(r)))
+        def _():
+            krylov_copy(r).start()
+
+        @pl.when(is_self(r))
+        def _():
+            for p in range(states):
+                krylov_ref[p, part] = out_send[r, p]
+
+    high, low = split(jnp.concatenate(last, axis=1))
+    gram = mm_t(high, high) + mm_t(high, low) + mm_t(low, high)
+    for r in range(2):
+        den_send[r] = float(sectors * width) * gram[r * rows:(r + 1) * rows]
+    for r in range(2):
+        @pl.when(jnp.logical_not(is_self(r)))
+        def _():
+            density_copy(r).start()
+
+        @pl.when(is_self(r))
+        def _():
+            den_got[part] = den_send[r]
+
+    for s in range(2):
+        @pl.when(jnp.logical_not(keeps & (s == 0)))
+        def _():
+            for which, src, dst in ((0, out_send.at[0], krylov_ref.at[:, s]), (1, den_send.at[0], den_got.at[s])):
+                pltpu.make_async_remote_copy(
+                    src_ref=src, dst_ref=dst,
+                    send_sem=out_ssem.at[which, 0], recv_sem=out_rsem.at[which, s],
+                    device_id=partner, device_id_type=MESH,
+                ).wait_recv()
+        rank = ranks_ref[s]
+        kept = (sub_ids < rank) & (col_ids < rank)
+        density_ref[s] = jnp.where(kept, den_got[s], 0.0)
+
+    for r in range(2):
+        @pl.when(jnp.logical_not(is_self(r)))
+        def _():
+            krylov_copy(r).wait_send()
+            density_copy(r).wait_send()
+    for j in range(3):
+        @pl.when(jnp.logical_not(keeps))
+        def _():
+            init_copy(0, j).wait_send()
+        init_copy(1, j).wait_send()
+    meta_copy.wait_send()
+
+
+def per_device_by_sector(start_vec, left_env, right_env, local_mpo, term_charge, sector_sizes, sector_ranks):
+    states, _, rows, width = start_vec.shape
+    terms = left_env.shape[0]
+    groups = lax.axis_size("blk") // 2
+    factors = jnp.concatenate([local_mpo.reshape(-1), term_charge.astype(F32)])
+    pad = -factors.shape[0] % 8
+    factors = jnp.pad(factors, (0, pad))
+    meta = jnp.broadcast_to(factors[:, None], (factors.shape[0], width))
+    block = (states, width, width)
+    dma = pltpu.SemaphoreType.DMA
+    vmem = pl.BlockSpec(memory_space=pltpu.VMEM)
+    smem = pl.BlockSpec(memory_space=pltpu.SMEM)
+
+    def kernel(*refs):
+        lanczos_kernel(groups, *refs)
+
+    return pl.pallas_call(
+        kernel,
+        out_shape=(
+            jax.ShapeDtypeStruct((2, KRY), F32),
+            jax.ShapeDtypeStruct(start_vec.shape, F32),
+            jax.ShapeDtypeStruct((2, rows, width), F32),
+        ),
+        in_specs=[vmem, vmem, vmem, vmem, smem, smem],
+        out_specs=(vmem, vmem, vmem),
+        scratch_shapes=[
+            pltpu.VMEM((2, states, rows, width), F32),
+            pltpu.VMEM((2, terms, width, width), F32),
+            pltpu.VMEM((2, terms, width, width), F32),
+            pltpu.VMEM((2, states, rows, width), F32),
+            pltpu.VMEM((2, terms, width, width), F32),
+            pltpu.VMEM((2, terms, width, width), F32),
+            pltpu.VMEM((2,) + meta.shape, F32),
+            pltpu.VMEM((2,) + block, F32),
+            pltpu.VMEM((2,) + block, F32),
+            pltpu.VMEM((2,) + block, F32),
+            pltpu.VMEM((2,) + block, F32),
+            pltpu.VMEM((2 * terms, width, 2 * width), BF),
+            pltpu.VMEM((2 * terms * width, 2 * width), BF),
+            pltpu.VMEM((2 * states * width, 2 * terms * width), BF),
+            pltpu.VMEM((states * width, width), F32),
+            pltpu.VMEM((2, 4, 8, width), F32),
+            pltpu.VMEM((2, groups, 8, width), F32),
+            pltpu.VMEM((8, width), F32),
+            pltpu.VMEM((2, states, rows, width), F32),
+            pltpu.VMEM((2, rows, width), F32),
+            pltpu.VMEM((2, rows, width), F32),
+            dma((2, 3)), dma((2, 3)), dma, dma,
+            dma((2,)), dma((2, 2)), dma((3,)), dma((2, 4)), dma((groups - 1,)), dma((2, groups)),
+            dma((2, 2)), dma((2, 2)),
+        ],
+        compiler_params=pltpu.CompilerParams(
+            collective_id=0, has_side_effects=True, vmem_limit_bytes=40 * 1024 * 1024
+        ),
+    )(start_vec, left_env, right_env, meta, sector_sizes, sector_ranks)
+
+
 def solution(mesh):
+    by_sector = mesh.shape["term"] == 2 and mesh.shape["blk"] % 2 == 0
     placed = (
         P(None, "blk", "term", None),
         P("term", "blk", None, None),
@@ -87,7 +563,7 @@
         P("blk"),
     )
     return jax.shard_map(
-        per_device,
+        per_device_by_sector if by_sector else per_device,
         mesh=mesh,
         in_specs=placed,
         out_specs=(P(), P(None, "blk", "term", None), P("blk", "term", None)),

time: 1150 us -> 120 us (0.10)
  blocking collectives: 744 us -> 0 us
  waiting for transfers between devices: 143 us -> 0 us
  matrix products: 126 us -> 0 us
  Pallas kernels: 0 us -> 112 us
  starting transfers between devices: 59.7 us -> 0 us
  other arithmetic: 30.5 us -> 0.08 us
  between operations: 26.6 us -> 0.67 us
    psum x17 -> x0, blocking collectives: 683 us -> none  [the longest x8 331 us: per_device(): norm_sq = lax.psum(jnp.sum(resid * resid), ('term', 'blk'))]
    dot_general x97 -> x0, matrix products: 126 us -> none  [the longest x32 51 us: apply_operator(): jnp.einsum('piac,ibc->piab', inner, right_env[term_idx], precision=HI)]
    reduce_scatter x8 -> x0, waiting for transfers between devices: 119 us -> none  [apply_operator(): lax.psum_scatter(partial_value, 'term', scatter_dimension=2, tiled=True)]
    pallas_call x0 -> x1, Pallas kernels: none -> 112 us  [per_device_by_sector(): pl.pallas_call(kernel, out_shape=(jax.ShapeDtypeStruct((2, KRY), F32), ja...]
    all_gather x9 -> x0, blocking collectives: 60.7 us -> none  [the longest x8 53.9 us: apply_operator(): whole = lax.all_gather(rows_vec, 'term', axis=2, tiled=True)]
    ppermute x16 -> x0, starting transfers between devices: 59.3 us -> none  [from_behind(): return lax.ppermute(value, axis, pairs)]
    reduce_sum x17 -> x0, other arithmetic: 26.3 us -> none  [the longest x8 13.7 us: per_device(): alpha = lax.psum(jnp.sum(vector * image), ('term', 'blk'))]
    ppermute x16 -> x0, waiting for transfers between devices: 23.8 us -> none  [from_behind(): return lax.ppermute(value, axis, pairs)]
  transfers between devices with their start and end apart: 24 -> 0, of which waited for: 22 -> 0; matrix products, arithmetic and copies ran while one was open for 0% -> 0% of each run, Pallas kernels for 0% -> 0%
where the time goes in v1:
time: 120 us; the launch traced here: 119 us
  Pallas kernels  112 us (93%)
  local copies, waits for them, and re-layouts  6.39 us (5%)
    pallas_call x1, Pallas kernels, per_device_by_sector(): pl.pallas_call(kernel, out_shape=(jax.ShapeDtypeStruct((2, KRY), F32), ja...  112 us
    unnamed x15, local copies, waits for them, and re-layouts  5.53 us

profile of v1, /device:TPU:1, one launch (start us, length us, event | category | flops | bytes accessed | tf_op | source)
XLA Modules:
  0.0 119.3 jit_solution(10084320566962530764)
XLA Ops:
  0.6 0.0 copy-start.5
  0.6 0.8 reshape.10
  1.4 0.0 copy-done.5
  1.5 0.1 fusion
  1.5 0.0 copy-start.3
  1.5 0.0 copy-start.4
  1.5 0.1 broadcast_in_dim.2.refs_3_
  1.6 0.6 copy-done.3
  2.2 0.0 copy-done.4
  2.2 0.0 copy-start
  2.2 1.0 copy-done
  3.2 0.0 copy-start.1
  3.2 1.0 copy-done.1
  4.3 0.0 copy-start.2
  4.3 0.9 copy-done.2
  5.2 112.2 %shard_map.94 = (f32[2,8]{1,0:T(2,128)S(1)}, f32[4,2,64,128]{3,2,1,0:T(8,128)S(1)}, f32[2,64,128]{2,1,0:T(8,128)S(1)}) custom-call(f32[4,2,64,128]{3,2,1,0:T(8,128)S(1)} %copy-done.2, f32[4,2,128,128]{3,2,1,0:T(8,128)S(1)} %copy-done, f32[4,2,128,128]{3,2,1,0:T(8,128)S(1)} %copy-done.1, f32[72,128]{1,0:T(8,128)S(1)} %broadcast_in_dim.2.refs_3_, ...), custom_call_target="tpu_custom_call" | custom-call | tf_op jit(solution)/shard_map/pallas_call | solution.py:513
  117.4 0.6 copy.13
  118.0 0.7 copy.14
  118.7 0.6 copy.15
  (1 shorter events, 0.0 us)
Async XLA Ops:
  0.6 0.8 copy-start.5
  1.5 0.7 copy-start.3
  1.5 0.7 copy-start.4
  2.2 1.0 copy-start
  3.2 1.0 copy-start.1
  4.3 0.9 copy-start.2

commit v2 on v1

--- a/solution.py
+++ b/solution.py
@@ -99,12 +99,12 @@
 
 def lanczos_kernel(
     groups,
-    start_ref, left_ref, right_ref, meta_ref, sizes_ref, ranks_ref,
+    start_ref, left_ref, right_ref, mpo_ref, charge_ref, sizes_ref, ranks_ref,
     coeffs_ref, krylov_ref, density_ref,
-    x_send, l_send, r_send, x_got, l_got, r_got, meta_got,
-    images, vectors, below, above,
+    meta_send_buf, counts_send, x_got, counts_got, l_got, r_got, meta_got,
+    images, vectors, below, above, from_below, from_above,
     l_split, r_split, mixed, applied,
-    pair_sums, all_sums, marks, out_send, den_send, den_got,
+    pair_sums, all_sums, marks, coefs, out_send, den_send,
     init_send, init_recv, meta_send, meta_recv,
     halo_send, halo_recv, pair_send, pair_recv, all_send, all_recv,
     out_ssem, out_rsem,
@@ -141,10 +141,8 @@
         other = (k + step) % groups
         return other, (t, other * 2 + c)
 
-    below[...] = jnp.zeros_like(below)
-    above[...] = jnp.zeros_like(above)
-    images[...] = jnp.zeros_like(images)
-    vectors[...] = jnp.zeros_like(vectors)
+    for ref in (below, above, from_below, from_above, images, vectors):
+        ref[...] = jnp.zeros_like(ref)
 
     barrier = pltpu.get_barrier_semaphore()
     for step in range(1, 4):
@@ -152,27 +150,31 @@
     for step in range(1, groups):
         pl.semaphore_signal(barrier, inc=1, device_id=group_dev(step)[1], device_id_type=MESH)
 
-    row_ids = lax.broadcasted_iota(jnp.int32, (width, width), 0)
-    col_ids = lax.broadcasted_iota(jnp.int32, (rows, width), 1)
-    sub_ids = lax.broadcasted_iota(jnp.int32, (rows, width), 0) + t * rows
+    for w in range(terms):
+        for p in range(states):
+            for q in range(states):
+                row = (w * states + p) * states + q
+                meta_send_buf[row:row + 1, :] = jnp.full((1, width), mpo_ref[w, p, q], F32)
+        row = terms * states * states + w
+        meta_send_buf[row:row + 1, :] = jnp.full((1, width), charge_ref[w].astype(F32), F32)
     for s in range(2):
-        size = sizes_ref[s]
-        live = (sub_ids < size) & (col_ids < size)
-        for p in range(states):
-            x_send[s, p] = jnp.where(live, start_ref[p, s], 0.0)
-        for w in range(terms):
-            l_send[s, w] = jnp.where(row_ids < size, left_ref[w, s], 0.0)
-            r_send[s, w] = jnp.where(row_ids < size, right_ref[w, s], 0.0)
+        counts_send[s, 0:1, :] = jnp.full((1, width), sizes_ref[s].astype(F32), F32)
+        counts_send[s, 1:8, :] = jnp.full((7, width), ranks_ref[s].astype(F32), F32)
 
     pl.semaphore_wait(barrier, 3 + groups - 1)
 
-    pieces = ((x_send, x_got), (l_send, l_got), (r_send, r_got))
+    pieces = (
+        (lambda s: start_ref.at[:, s], x_got),
+        (lambda s: counts_send.at[s], counts_got),
+        (lambda s: left_ref.at[:, s], l_got),
+        (lambda s: right_ref.at[:, s], r_got),
+    )
     target_t = (c + flip) % 2
 
     def init_copy(s, j):
         src, dst = pieces[j]
         return pltpu.make_async_remote_copy(
-            src_ref=src.at[s], dst_ref=dst.at[t],
+            src_ref=src(s), dst_ref=dst.at[t],
             send_sem=init_send.at[s, j], recv_sem=init_recv.at[t, j],
             device_id=(target_t, k * 2 + (s + c) % 2), device_id_type=MESH,
         )
@@ -180,39 +182,48 @@
     keeps = target_t == t
     partner = pair_dev(2)[1]
     meta_copy = pltpu.make_async_remote_copy(
-        src_ref=meta_ref, dst_ref=meta_got.at[t],
+        src_ref=meta_send_buf, dst_ref=meta_got.at[t],
         send_sem=meta_send, recv_sem=meta_recv,
         device_id=partner, device_id_type=MESH,
     )
-    for j in range(3):
+    def own_copy(j):
+        src, dst = pieces[j]
+        return pltpu.make_async_copy(src(0), dst.at[t], init_recv.at[t, j])
+
+    for j in range(4):
         @pl.when(jnp.logical_not(keeps))
         def _():
             init_copy(0, j).start()
+
+        @pl.when(keeps)
+        def _():
+            own_copy(j).start()
+
         init_copy(1, j).start()
-        if j == 0:
+        if j == 1:
             meta_copy.start()
 
-    @pl.when(keeps)
-    def _():
-        x_got[t] = x_send[0]
-        l_got[t] = l_send[0]
-        r_got[t] = r_send[0]
-
-    meta_got[t] = meta_ref[...]
+    meta_got[t] = meta_send_buf[...]
 
     def init_wait(source, j):
         src, dst = pieces[j]
-        @pl.when(jnp.logical_not((source == t) & (half == c)))
-        def _():
-            pltpu.make_async_remote_copy(
-                src_ref=src.at[0], dst_ref=dst.at[source],
-                send_sem=init_send.at[0, j], recv_sem=init_recv.at[source, j],
-                device_id=partner, device_id_type=MESH,
-            ).wait_recv()
-
+        pltpu.make_async_remote_copy(
+            src_ref=src(0), dst_ref=dst.at[source],
+            send_sem=init_send.at[0, j], recv_sem=init_recv.at[source, j],
+            device_id=partner, device_id_type=MESH,
+        ).wait_recv()
+
+    row_ids = lax.broadcasted_iota(jnp.int32, (width, width), 0).astype(F32)
+    col_ids = lax.broadcasted_iota(jnp.int32, (width, width), 1).astype(F32)
     for source in range(2):
         init_wait(source, 0)
-        images[0, :, pl.ds(source * rows, rows), :] = x_got[source]
+        init_wait(source, 1)
+        size = counts_got[source, 0:1, :]
+        at = source * rows
+        live = (row_ids[at:at + rows] < size) & (col_ids[:rows] < size)
+        for p in range(states):
+            applied[p, pl.ds(at, rows), :] = jnp.where(live, x_got[source, p], 0.0)
+    live_rows = row_ids < counts_got[0, 0:1, :]
 
     def lane_sums(first, second):
         total = first[0] * second[0]
@@ -274,7 +285,7 @@
         total = all_sums[slot, 0]
         for other in range(1, groups):
             total = total + all_sums[slot, other]
-        dots = jnp.sum(total, axis=1, keepdims=True)
+        dots = jnp.broadcast_to(jnp.sum(total, axis=1, keepdims=True), total.shape)
         ww, vw, uw, vv, uv, uu = (dots[i:i + 1] for i in range(6))
         alpha = vw
         norm_sq = (
@@ -289,73 +300,75 @@
             group_copy(slot, step).wait_send()
         return alpha, beta
 
-    def down_copy(slot):
-        return pltpu.make_async_remote_copy(
-            src_ref=images.at[slot], dst_ref=above.at[slot],
-            send_sem=halo_send.at[0], recv_sem=halo_recv.at[slot, 0],
+    chunk = states // 2
+
+    def down_copy(slot, part_of):
+        span = pl.ds(part_of * chunk, chunk)
+        return pltpu.make_async_remote_copy(
+            src_ref=applied.at[span], dst_ref=from_above.at[slot, span],
+            send_sem=halo_send.at[0, part_of], recv_sem=halo_recv.at[slot, 0, part_of],
             device_id=lower_dev, device_id_type=MESH,
         )
 
-    def up_copy(slot):
-        return pltpu.make_async_remote_copy(
-            src_ref=images.at[slot], dst_ref=below.at[slot],
-            send_sem=halo_send.at[1], recv_sem=halo_recv.at[slot, 1],
+    def up_copy(slot, part_of):
+        span = pl.ds(part_of * chunk, chunk)
+        return pltpu.make_async_remote_copy(
+            src_ref=applied.at[span], dst_ref=from_below.at[slot, span],
+            send_sem=halo_send.at[1, part_of], recv_sem=halo_recv.at[slot, 1, part_of],
             device_id=upper_dev, device_id_type=MESH,
         )
 
-    def start_halo(slot):
+    def start_halo(slot, part_of):
         @pl.when(has_lower)
         def _():
-            down_copy(slot).start()
+            down_copy(slot, part_of).start()
 
         @pl.when(has_upper)
         def _():
-            up_copy(slot).start()
-
-    def wait_halo(slot):
+            up_copy(slot, part_of).start()
+
+    def wait_halo(slot, part_of):
         @pl.when(has_lower)
         def _():
-            up_copy(slot).wait_recv()
+            up_copy(slot, part_of).wait_recv()
 
         @pl.when(has_upper)
         def _():
-            down_copy(slot).wait_recv()
-
-    def wait_halo_send(slot):
+            down_copy(slot, part_of).wait_recv()
+
+    def wait_halo_send(slot, part_of):
         @pl.when(has_lower)
         def _():
-            down_copy(slot).wait_send()
+            down_copy(slot, part_of).wait_send()
 
         @pl.when(has_upper)
         def _():
-            up_copy(slot).wait_send()
-
-    start_halo(0)
-    first = images[0]
-    write_products(0, first, vectors[0], vectors[1])
-    start_pair(0)
+            up_copy(slot, part_of).wait_send()
+
+    for part_of in range(2):
+        start_halo(0, part_of)
 
     meta_copy.wait_recv()
-    for source in range(2):
-        init_wait(source, 1)
-        for w in range(terms):
-            high, low = split(l_got[source, w])
-            l_split[source * terms + w] = jnp.concatenate([high, low], axis=1)
     for source in range(2):
         init_wait(source, 2)
         for w in range(terms):
-            high, low = split(r_got[source, w].T)
+            high, low = split(jnp.where(live_rows, l_got[source, w], 0.0))
+            l_split[source * terms + w] = jnp.concatenate([high, low], axis=1)
+    for source in range(2):
+        init_wait(source, 3)
+        for w in range(terms):
+            high, low = split(jnp.where(live_rows, r_got[source, w], 0.0).T)
             r_split[pl.ds((source * terms + w) * width, width), :] = jnp.concatenate([high, low], axis=1)
 
-    def apply(slot):
+    def apply(slot, send):
         for w in range(2 * terms):
             source, local = w // terms, w % terms
             charge = meta_got[source, pl.ds(states * states * terms + local, 1), :]
-            from_below = charge > 0.5
-            from_above = charge < -0.5
+            is_below = charge > 0.5
+            is_above = charge < -0.5
             vec = jnp.concatenate(
                 [
-                    jnp.where(from_below, below[slot, q], jnp.where(from_above, above[slot, q], images[slot, q]))
+                    jnp.where(is_below, below[slot, q], jnp.where(is_above, above[slot, q], images[slot, q]))
                     for q in range(states)
                 ],
                 axis=1,
@@ -374,9 +387,17 @@
                 mixed[pl.ds(p * width, width), pl.ds(w * width, width)] = high
                 mixed[pl.ds((states + p) * width, width), pl.ds(w * width, width)] = low
         stacked = states * width
-        top = mm(mixed[pl.ds(0, stacked), :], r_split[...])
-        bottom = mm(mixed[pl.ds(stacked, stacked), :], r_split[:, :width])
-        applied[...] = top[:, :width] + top[:, width:] + bottom
+        span = chunk * width
+        for part_of in range(2):
+            top = mm(mixed[pl.ds(part_of * span, span), :], r_split[...])
+            bottom = mm(mixed[pl.ds(stacked + part_of * span, span), :], r_split[:, :width])
+            result = top[:, :width] + top[:, width:] + bottom
+            for p in range(chunk):
+                applied[part_of * chunk + p] = result[p * width:(p + 1) * width]
+
+            @pl.when(send)
+            def _():
+                start_halo(1 - slot, part_of)
 
     lanes = lax.broadcasted_iota(jnp.int32, marks.shape, 1)
     subs = lax.broadcasted_iota(jnp.int32, marks.shape, 0)
@@ -386,35 +407,45 @@
         here = lanes == index
         marks[...] = jnp.where(here & (subs == 0), alpha, jnp.where(here & (subs == 1), beta, marks[...]))
 
-    def step_body(it, beta_before):
+    def advance(slot, alpha, beta_before, scale):
+        other = 1 - slot
+        for p in range(states):
+            image = images[other, p]
+            vectors[slot, p] = (image - alpha * vectors[other, p] - beta_before * vectors[slot, p]) * scale
+            images[slot, p] = (applied[p] - alpha * image - beta_before * images[slot, p]) * scale
+        write_products(slot, images[slot], vectors[slot], vectors[other])
+        start_pair(slot)
+
+    def step_body(it, carry):
+        alpha, beta_before, beta_next, scale = (coefs[i:i + 1, :] for i in range(4))
         slot = it % 2
         other = 1 - slot
-        wait_halo(slot)
+        advance(slot, alpha, beta_before, scale)
         finish_pair(slot)
-        apply(slot)
-        alpha, beta = finish_sums(slot, beta_before)
+        for part_of in range(2):
+            wait_halo(slot, part_of)
+            for p in range(part_of * chunk, (part_of + 1) * chunk):
+                for edge, got in ((below, from_below), (above, from_above)):
+                    edge[slot, p] = (got[slot, p] - alpha * edge[other, p] - beta_before * edge[slot, p]) * scale
+            wait_halo_send(slot, part_of)
+        apply(slot, it < KRY - 1)
+        alpha, beta = finish_sums(slot, beta_next)
         record(it - 1, alpha, beta)
-        scale = 1.0 / beta
-        for p in range(states):
-            image = images[slot, p]
-            vector = vectors[slot, p]
-            done = applied[pl.ds(p * width, width), :]
-            vectors[other, p] = (image - alpha * vector - beta_before * vectors[other, p]) * scale
-            images[other, p] = (done - alpha * image - beta_before * images[other, p]) * scale
-        wait_halo_send(slot)
-
-        @pl.when(it < KRY - 1)
-        def _():
-            start_halo(other)
-
-        write_products(other, images[other], vectors[other], vectors[slot])
-        start_pair(other)
-        return jnp.where(it == 0, 0.0, beta)
-
-    beta_before = lax.fori_loop(0, KRY, step_body, jnp.zeros((1, 1), F32))
+        coefs[0:1, :] = alpha
+        coefs[1:2, :] = beta_next
+        coefs[2:3, :] = jnp.where(it == 0, 0.0, beta)
+        coefs[3:4, :] = 1.0 / beta
+        return carry
+
+    coefs[0:3, :] = jnp.zeros((3, width), F32)
+    coefs[3:4, :] = jnp.ones((1, width), F32)
+    lax.fori_loop(0, KRY, step_body, 0)
+    alpha, beta_before, beta_next, scale = (coefs[i:i + 1, :] for i in range(4))
     slot = KRY % 2
+    advance(slot, alpha, beta_before, scale)
     finish_pair(slot)
-    alpha, beta = finish_sums(slot, beta_before)
+    alpha, beta = finish_sums(slot, beta_next)
+    beta_before = beta_next
     record(KRY - 1, alpha, beta)
     coeffs_ref[...] = marks[:2, :KRY]
     scale = 1.0 / beta
@@ -437,7 +468,7 @@
 
     def density_copy(r):
         return pltpu.make_async_remote_copy(
-            src_ref=den_send.at[r], dst_ref=den_got.at[part],
+            src_ref=den_send.at[r], dst_ref=density_ref.at[part],
             send_sem=out_ssem.at[1, r], recv_sem=out_rsem.at[1, part],
             device_id=(r, k * 2 + half), device_id_type=MESH,
         )
@@ -452,13 +483,14 @@
 
         @pl.when(is_self(r))
         def _():
-            for p in range(states):
-                krylov_ref[p, part] = out_send[r, p]
+            pltpu.make_async_copy(out_send.at[r], krylov_ref.at[:, part], out_rsem.at[0, part]).start()
 
     high, low = split(jnp.concatenate(last, axis=1))
     gram = mm_t(high, high) + mm_t(high, low) + mm_t(low, high)
+    rank = counts_got[0, 1:2, :]
+    gram = jnp.where((row_ids < rank) & (col_ids < rank), float(sectors * width) * gram, 0.0)
     for r in range(2):
-        den_send[r] = float(sectors * width) * gram[r * rows:(r + 1) * rows]
+        den_send[r] = gram[r * rows:(r + 1) * rows]
     for r in range(2):
         @pl.when(jnp.logical_not(is_self(r)))
         def _():
@@ -466,27 +498,22 @@
 
         @pl.when(is_self(r))
         def _():
-            den_got[part] = den_send[r]
+            pltpu.make_async_copy(den_send.at[r], density_ref.at[part], out_rsem.at[1, part]).start()
 
     for s in range(2):
-        @pl.when(jnp.logical_not(keeps & (s == 0)))
-        def _():
-            for which, src, dst in ((0, out_send.at[0], krylov_ref.at[:, s]), (1, den_send.at[0], den_got.at[s])):
-                pltpu.make_async_remote_copy(
-                    src_ref=src, dst_ref=dst,
-                    send_sem=out_ssem.at[which, 0], recv_sem=out_rsem.at[which, s],
-                    device_id=partner, device_id_type=MESH,
-                ).wait_recv()
-        rank = ranks_ref[s]
-        kept = (sub_ids < rank) & (col_ids < rank)
-        density_ref[s] = jnp.where(kept, den_got[s], 0.0)
+        for which, src, dst in ((0, out_send.at[0], krylov_ref.at[:, s]), (1, den_send.at[0], density_ref.at[s])):
+            pltpu.make_async_remote_copy(
+                src_ref=src, dst_ref=dst,
+                send_sem=out_ssem.at[which, 0], recv_sem=out_rsem.at[which, s],
+                device_id=partner, device_id_type=MESH,
+            ).wait_recv()
 
     for r in range(2):
         @pl.when(jnp.logical_not(is_self(r)))
         def _():
             krylov_copy(r).wait_send()
             density_copy(r).wait_send()
-    for j in range(3):
+    for j in range(4):
         @pl.when(jnp.logical_not(keeps))
         def _():
             init_copy(0, j).wait_send()
@@ -498,14 +525,13 @@
     states, _, rows, width = start_vec.shape
     terms = left_env.shape[0]
     groups = lax.axis_size("blk") // 2
-    factors = jnp.concatenate([local_mpo.reshape(-1), term_charge.astype(F32)])
-    pad = -factors.shape[0] % 8
-    factors = jnp.pad(factors, (0, pad))
-    meta = jnp.broadcast_to(factors[:, None], (factors.shape[0], width))
+    meta_rows = terms * states * states + terms
+    meta_rows += -meta_rows % 8
     block = (states, width, width)
     dma = pltpu.SemaphoreType.DMA
     vmem = pl.BlockSpec(memory_space=pltpu.VMEM)
     smem = pl.BlockSpec(memory_space=pltpu.SMEM)
+    hbm = pl.BlockSpec(memory_space=pltpu.HBM)
 
     def kernel(*refs):
         lanczos_kernel(groups, *refs)
@@ -517,16 +543,18 @@
             jax.ShapeDtypeStruct(start_vec.shape, F32),
             jax.ShapeDtypeStruct((2, rows, width), F32),
         ),
-        in_specs=[vmem, vmem, vmem, vmem, smem, smem],
-        out_specs=(vmem, vmem, vmem),
+        in_specs=[hbm, hbm, hbm, smem, smem, smem, smem],
+        out_specs=(vmem, hbm, hbm),
         scratch_shapes=[
+            pltpu.VMEM((meta_rows, width), F32),
+            pltpu.VMEM((2, 8, width), F32),
             pltpu.VMEM((2, states, rows, width), F32),
+            pltpu.VMEM((2, 8, width), F32),
             pltpu.VMEM((2, terms, width, width), F32),
             pltpu.VMEM((2, terms, width, width), F32),
-            pltpu.VMEM((2, states, rows, width), F32),
-            pltpu.VMEM((2, terms, width, width), F32),
-            pltpu.VMEM((2, terms, width, width), F32),
-            pltpu.VMEM((2,) + meta.shape, F32),
+            pltpu.VMEM((2, meta_rows, width), F32),
+            pltpu.VMEM((2,) + block, F32),
+            pltpu.VMEM((2,) + block, F32),
             pltpu.VMEM((2,) + block, F32),
             pltpu.VMEM((2,) + block, F32),
             pltpu.VMEM((2,) + block, F32),
@@ -534,21 +562,21 @@
             pltpu.VMEM((2 * terms, width, 2 * width), BF),
             pltpu.VMEM((2 * terms * width, 2 * width), BF),
             pltpu.VMEM((2 * states * width, 2 * terms * width), BF),
-            pltpu.VMEM((states * width, width), F32),
+            pltpu.VMEM(block, F32),
             pltpu.VMEM((2, 4, 8, width), F32),
             pltpu.VMEM((2, groups, 8, width), F32),
             pltpu.VMEM((8, width), F32),
+            pltpu.VMEM((8, width), F32),
             pltpu.VMEM((2, states, rows, width), F32),
             pltpu.VMEM((2, rows, width), F32),
-            pltpu.VMEM((2, rows, width), F32),
-            dma((2, 3)), dma((2, 3)), dma, dma,
-            dma((2,)), dma((2, 2)), dma((3,)), dma((2, 4)), dma((groups - 1,)), dma((2, groups)),
+            dma((2, 4)), dma((2, 4)), dma, dma,
+            dma((2, 2)), dma((2, 2, 2)), dma((3,)), dma((2, 4)), dma((groups - 1,)), dma((2, groups)),
             dma((2, 2)), dma((2, 2)),
         ],
         compiler_params=pltpu.CompilerParams(
             collective_id=0, has_side_effects=True, vmem_limit_bytes=40 * 1024 * 1024
         ),
-    )(start_vec, left_env, right_env, meta, sector_sizes, sector_ranks)
+    )(start_vec, left_env, right_env, local_mpo, term_charge, sector_sizes, sector_ranks)
 
 
 def solution(mesh):

time: 120 us -> 106 us (0.88)
  Pallas kernels: 112 us -> 97.5 us
    pallas_call x1, Pallas kernels: 112 us -> 97.5 us  [per_device_by_sector(): pl.pallas_call(kernel, out_shape=(jax.ShapeDtypeStruct((2, KRY), F32), ja...]
    unnamed x15 -> x17, local copies, waits for them, and re-layouts: 5.53 us -> 7.58 us
where the time goes in v2:
time: 106 us
  Pallas kernels  97.5 us (92%)
  local copies, waits for them, and re-layouts  7.58 us (7%)
    pallas_call x1, Pallas kernels, per_device_by_sector(): pl.pallas_call(kernel, out_shape=(jax.ShapeDtypeStruct((2, KRY), F32), ja...  97.5 us
    unnamed x17, local copies, waits for them, and re-layouts  7.58 us

profile of v2, /device:TPU:1, one launch (start us, length us, event | category | flops | bytes accessed | tf_op | source)
XLA Modules:
  0.0 105.8 jit_solution(13694014588829329957)
XLA Ops:
  0.6 0.0 copy-start
  0.6 1.0 copy-done
  1.7 0.0 copy-start.1
  1.7 1.0 copy-done.1
  2.7 0.0 copy-start.2
  2.7 0.9 copy-done.2
  3.7 0.0 copy-start.3
  3.7 0.7 copy-done.3
  4.4 0.0 copy-start.4
  4.4 0.7 copy-done.4
  5.0 0.0 copy-start.5
  5.0 0.7 copy-done.5
  5.7 0.0 copy-start.6
  5.7 0.7 copy-done.6
  6.3 97.5 %shard_map.94 = (f32[2,8]{1,0:T(2,128)S(1)}, f32[4,2,64,128]{3,2,1,0:T(8,128)S(1)}, f32[2,64,128]{2,1,0:T(8,128)S(1)}) custom-call(f32[4,2,64,128]{3,2,1,0:T(8,128)S(1)} %copy-done.2, f32[4,2,128,128]{3,2,1,0:T(8,128)S(1)} %copy-done, f32[4,2,128,128]{3,2,1,0:T(8,128)S(1)} %copy-done.1, f32[4,4,4]{2,1,0:T(4,128)S(1)} %copy-done.3, s32[4]{0:T(128)S(1)} %copy-done.4, ...), custom_call_target="tpu_custom_call" | custom-call | tf_op jit(solution)/shard_map/pallas_call | solution.py:539
  103.9 0.6 copy.13
  104.5 0.7 copy.14
  105.2 0.6 copy.15
Async XLA Ops:
  0.6 1.0 copy-start
  1.7 1.0 copy-start.1
  2.7 0.9 copy-start.2
  3.7 0.7 copy-start.3
  4.4 0.7 copy-start.4
  5.0 0.7 copy-start.5
  5.7 0.7 copy-start.6

commit v3 on v2

--- a/solution.py
+++ b/solution.py
@@ -574,7 +574,7 @@
             dma((2, 2)), dma((2, 2)),
         ],
         compiler_params=pltpu.CompilerParams(
-            collective_id=0, has_side_effects=True, vmem_limit_bytes=40 * 1024 * 1024
+            collective_id=0, has_side_effects=True, vmem_limit_bytes=63 * 1024 * 1024
         ),
     )(start_vec, left_env, right_env, local_mpo, term_charge, sector_sizes, sector_ranks)
 

time: 106 us -> 103 us (0.972)
  local copies, waits for them, and re-layouts: 7.58 us -> 3.53 us
  Pallas kernels: 97.5 us -> 98.6 us
    unnamed x17 -> x7, local copies, waits for them, and re-layouts: 7.58 us -> 3.53 us
where the time goes in v3:
time: 103 us
  Pallas kernels  98.6 us (96%)
  local copies, waits for them, and re-layouts  3.53 us (3%)
    pallas_call x1, Pallas kernels, per_device_by_sector(): pl.pallas_call(kernel, out_shape=(jax.ShapeDtypeStruct((2, KRY), F32), ja...  98.6 us
    unnamed x7, local copies, waits for them, and re-layouts  3.53 us

profile of v3, /device:TPU:1, one launch (start us, length us, event | category | flops | bytes accessed | tf_op | source)
XLA Modules:
  0.0 102.8 jit_solution(3459185437717882341)
XLA Ops:
  0.6 98.6 %shard_map.94 = (f32[2,8]{1,0:T(2,128)}, f32[4,2,64,128]{3,2,1,0:T(8,128)}, f32[2,64,128]{2,1,0:T(8,128)}) custom-call(f32[4,2,64,128]{3,2,1,0:T(8,128)} %refs_0_.1, f32[4,2,128,128]{3,2,1,0:T(8,128)} %refs_1_.1, f32[4,2,128,128]{3,2,1,0:T(8,128)} %refs_2_.1, f32[4,4,4]{2,1,0:T(4,128)} %refs_3_.1, s32[4]{0:T(128)} %refs_4_.1, s32[2]{0:T(128)} %refs_5_.1, ...), custom_call_target="tpu_custom_call" | custom-call | tf_op jit(solution)/shard_map/pallas_call | solution.py:539
  99.2 0.0 copy-start.1
  99.2 0.6 copy-done.1
  99.9 0.6 copy.13
  100.4 0.0 copy-start
  100.4 1.7 %copy.14 = f32[4,2,64,128]{3,2,1,0:T(8,128)} copy(f32[4,2,64,128]{3,2,1,0:T(8,128)} %get-tuple-element.7) | data formatting | bytes 524288
  102.1 0.0 copy-done
  102.1 0.6 copy.15
Async XLA Ops:
  99.2 0.6 copy-start.1
  100.4 1.7 %copy-start = (f32[2,64,128]{2,1,0:T(8,128)S(1)}, f32[2,64,128]{2,1,0:T(8,128)}, u32[]{:S(2)}) copy-start(f32[2,64,128]{2,1,0:T(8,128)} %get-tuple-element.8) | copy-start | bytes 196612
